TPU v7x, 256 devices: a whole 4x4x8 slice. The times are simulated.
256 devices in a mesh: blk: 64 (over x, y, z_lo, core), head: 4 (over z_hi).
Axes of the slice: x: 4, y: 4, z: 8 (z_hi: 4, z_lo: 2; z = z_hi * 2 + z_lo), core: 2. Of those that a mesh axis runs over, the one named last changes fastest.
Arguments:
- queries: bfloat16 [16384, 4096], P(('blk', 'head')), may hold values from -6 to 6
- keys: bfloat16 [16384, 512], P(('blk', 'head')), may hold values from -6 to 6
- values: bfloat16 [16384, 512], P(('blk', 'head')), may hold values from -6 to 6
- positions: int32 [16384], P(('blk', 'head')), may hold values from 0 to 16383, as said below
Outputs:
- attended: bfloat16 [16384, 4096], P(('blk', 'head'))
Inputs may be any that keep to these rules, and one draw needn't show every extreme that they name: Positions are distinct. The rows fall into spans of 128 rows holding consecutive rising positions that start at a multiple of 128; the two spans of one index of blk are span j and span 2 * 64 - 1 - j of the document, each j at exactly one index. Positions are integer bookkeeping: any lossless encoding of them between devices is allowed.
All inputs are finite; a program needn't handle non-finite values.
Results may differ from a plain program's by a relative error of at most 0.0083.
Values may be sent and summed in bfloat16 or wider, within the bound.
A program may use at most 128 MiB of HBM per device.

v0:
```python
import math

import jax
import jax.numpy as jnp
import numpy as np
from jax import lax
from jax.sharding import PartitionSpec as P

QHEADS = 32
KVHEADS = 4
HEAD_DIM = 128


def rope_table(size):
    entries = []
    for number in range(size // 2):
        inverse = 1.0 / 500000.0 ** (2.0 * number / size)
        wavelength = 2.0 * math.pi / inverse
        if wavelength < 2048.0:
            entries.append(inverse)
        elif wavelength > 8192.0:
            entries.append(inverse / 8.0)
        else:
            smooth = (8192.0 / wavelength - 1.0) / 3.0
            entries.append((1.0 - smooth) * inverse / 8.0 + smooth * inverse)
    return np.array(entries, dtype=np.float32)


def rotate(inputs, places, head_count):
    size = inputs.shape[1] // head_count
    table = jnp.asarray(rope_table(size))
    angles = places.astype(jnp.float32)[:, None] * table[None, :]
    cosine = jnp.cos(angles)[:, None, :]
    sine = jnp.sin(angles)[:, None, :]
    shaped = inputs.astype(jnp.float32).reshape(inputs.shape[0], head_count, size)
    half_size = size // 2
    first = shaped[:, :, :half_size]
    second = shaped[:, :, half_size:]
    turned = jnp.concatenate(
        [first * cosine - second * sine, second * cosine + first * sine], axis=2
    )
    return turned.reshape(inputs.shape).astype(jnp.bfloat16)


def attend(state, query_rows, query_places, key_rows, value_rows, key_places, scale):
    maximum, total, summed = state
    scores = (
        jnp.einsum("qgrd,kgd->grqk", query_rows, key_rows, preferred_element_type=jnp.float32)
        * scale
    )
    visible = key_places[None, None, None, :] <= query_places[None, None, :, None]
    newest = jnp.maximum(maximum, jnp.max(jnp.where(visible, scores, -1e30), axis=3))
    factor = jnp.exp(maximum - newest)
    weights = jnp.where(visible, jnp.exp(scores - newest[..., None]), 0.0)
    total = total * factor + jnp.sum(weights, axis=3)
    summed = summed * factor[..., None] + jnp.einsum(
        "grqk,kgd->grqd",
        weights.astype(jnp.bfloat16),
        value_rows,
        preferred_element_type=jnp.float32,
    )
    return (newest, total, summed)


def start_state(query_rows):
    row_count, groups, group_size, head_size = query_rows.shape
    maximum = jnp.full((groups, group_size, row_count), -1e30, jnp.float32)
    total = jnp.zeros((groups, group_size, row_count), jnp.float32)
    summed = jnp.zeros((groups, group_size, row_count, head_size), jnp.float32)
    return (maximum, total, summed)


def make_fold(query_rows, query_places, all_places, span_rows, scale):
    row_count, groups, group_size, head_size = query_rows.shape
    sub_rows = min(row_count, span_rows)
    sub_count = row_count // sub_rows
    sub_highest = [
        jnp.max(query_places[index * sub_rows : (index + 1) * sub_rows])
        for index in range(sub_count)
    ]

    def fold(state, pieces, start):
        key_part, value_part = pieces
        count = key_part.shape[0]
        key_part = key_part.reshape(count, groups, head_size)
        value_part = value_part.reshape(count, groups, head_size)
        step_rows = math.gcd(count, 2048)

        def inner(index, carry):
            begin = index * step_rows
            key_block = lax.dynamic_slice_in_dim(key_part, begin, step_rows, 0)
            value_block = lax.dynamic_slice_in_dim(value_part, begin, step_rows, 0)
            key_places = lax.dynamic_slice_in_dim(all_places, begin, step_rows, 0)
            lowest = jnp.min(key_places)
            updates = []
            for sub_index in range(sub_count):
                lower = sub_index * sub_rows
                upper = lower + sub_rows
                carry_part = tuple((item[:, :, lower:upper] for item in carry))
                rows_part = query_rows[lower:upper]
                places_sub = query_places[lower:upper]
                updates.append(
                    lax.cond(
                        lowest <= sub_highest[sub_index],
                        lambda inner_state: attend(
                            inner_state,
                            rows_part,
                            places_sub,
                            key_block,
                            value_block,
                            key_places,
                            scale,
                        ),
                        lambda inner_state: inner_state,
                        carry_part,
                    )
                )
            return tuple(
                (
                    jnp.concatenate([update[member] for update in updates], axis=2)
                    for member in range(3)
                )
            )

        return lax.fori_loop(0, count // step_rows, inner, state)

    return fold


def finish(state):
    maximum, total, summed = state
    normed = summed / total[..., None]
    ordered = jnp.transpose(normed, (2, 0, 1, 3))
    return ordered.reshape(ordered.shape[0], -1).astype(jnp.bfloat16)


def body(queries, keys, values, positions):
    token_rows = queries.shape[0]
    group_size = QHEADS // KVHEADS
    scale = HEAD_DIM ** (-0.5)
    span_rows = lax.axis_size("head") * token_rows // 2
    q_rot = rotate(queries, positions, QHEADS)
    k_rot = rotate(keys, positions, KVHEADS)
    all_places = lax.all_gather(positions, ("blk", "head"), axis=0, tiled=True)
    q_here, k_here, v_here = (
        lax.all_to_all(q_rot, "head", split_axis=1, concat_axis=0, tiled=True),
        lax.all_to_all(k_rot, "head", split_axis=1, concat_axis=0, tiled=True),
        lax.all_to_all(values, "head", split_axis=1, concat_axis=0, tiled=True),
    )
    row_count = q_here.shape[0]
    groups = k_here.shape[1] // HEAD_DIM
    query_rows = q_here.reshape(row_count, groups, group_size, HEAD_DIM)
    query_places = lax.dynamic_slice_in_dim(
        all_places, lax.axis_index("blk") * row_count, row_count, 0
    )
    folder = make_fold(query_rows, query_places, all_places, span_rows, scale)
    final_state = folder(
        start_state(query_rows),
        (
            lax.all_gather(k_here, "blk", axis=0, tiled=True),
            lax.all_gather(v_here, "blk", axis=0, tiled=True),
        ),
        jnp.int32(0),
    )
    mixed = finish(final_state)
    return lax.all_to_all(mixed, "head", split_axis=0, concat_axis=1, tiled=True)


def solution(mesh):
    return jax.shard_map(
        body,
        mesh=mesh,
        in_specs=(
            P(("blk", "head"), None),
            P(("blk", "head"), None),
            P(("blk", "head"), None),
            P(("blk", "head")),
        ),
        out_specs=P(("blk", "head"), None),
        check_vma=False,
    )
```

profile of v0, /device:TPU:18, one launch (start us, length us, event | category | flops | bytes accessed | tf_op | source)
XLA Modules:
  0.0 439.6 jit_solution(12476111983824867983)
XLA Ops:
  8.8 8.5 %all-to-all-start.1 = ((bf16[64,4,128]{2,0,1:T(8,128)(2,1)}), bf16[64,4,128]{2,0,1:T(8,128)(2,1)S(1)}, u32[]{:S(2)}, u32[]{:S(2)}) async-start(bf16[64,4,128]{2,0,1:T(8,128)(2,1)} %copy_bitcast_fusion), calls=%async_computation.1 | async-start | bytes 131072 | tf_op jit(solution)/shard_map/all_to_all | solution.py:148
  18.9 6.6 %all-to-all-done.1 = bf16[64,4,128]{2,0,1:T(8,128)(2,1)S(1)} async-done(((bf16[64,4,128]{2,0,1:T(8,128)(2,1)}), bf16[64,4,128]{2,0,1:T(8,128)(2,1)S(1)}, u32[]{:S(2)}, u32[]{:S(2)}) %all-to-all-start.1) | async-done | bytes 65568 | tf_op jit(solution)/shard_map/all_to_all | solution.py:148
  28.9 11.2 %all_to_all.64 = bf16[64,4,128]{2,0,1:T(8,128)(2,1)} all-to-all(bf16[64,4,128]{2,0,1:T(8,128)(2,1)S(1)} %pad_maximum_fusion.4), channel_id=1, replica_groups=mesh['blk'=64,'head'=4] {'head'}, dimensions={1} | all-to-all | bytes 131072 | tf_op jit(solution)/shard_map/all_to_all | solution.py:147
  43.4 3.5 all-to-all-start.2
  46.9 219.0 %all-reduce.3.cloned.1.call-done = s32[16384]{0:T(1024)} async-done(((s32[16384]{0:T(1024)}), s32[16384]{0:T(1024)}) %all-reduce.3.cloned.1.call-update) | async-done | bytes 65552
  267.6 142.9 %while.17 = (s32[]{:T(128)}, f32[1,8,256]{2,1,0:T(8,128)S(1)}, f32[1,8,256]{2,1,0:T(8,128)S(1)}, f32[1,8,256,128]{3,2,1,0:T(8,128)S(1)}, s32[16384]{0:T(1024)}, ...) while((s32[]{:T(128)}, f32[1,8,256]{2,1,0:T(8,128)S(1)}, ...), condition=%wide.region_12.13_spmd, body=%wide.region_2.12_spmd.sunk | while | flops 2194944000 | bytes 67866120 | solution.py:125
  273.8 5.9 %conditional.4 = ((f32[1,8,128]{2,1,0:T(8,128)S(1)}, f32[1,8,128]{2,1,0:T(8,128)S(1)}, f32[1,8,128,128]{3,2,1,0:T(8,128)S(1)})) conditional(s32[]{:T(128)} %convert_element_type.69, (f32[1,8,128]{2,1,0:T(8,128)S(1)}, f32[1,8,128]{2,1,0:T(8,128)S(1)}, f32[1,8,128,128]{3,2,1,0:T(8,128)S(1)}) %tuple.73, (s32[2048]{0:T(1024)S(1)}, s32[256]{0:T(256)S(1)}, ...), branch_computations={%region_8.8_spmd, %region_9.11_spmd} | conditional | flops 1097337856 | bytes 30746172 | solution.py:103
  275.6 2.3 fusion.35
  279.7 5.9 %conditional.5 = ((f32[1,8,128]{2,1,0:T(8,128)S(1)}, f32[1,8,128]{2,1,0:T(8,128)S(1)}, f32[1,8,128,128]{3,2,1,0:T(8,128)S(1)})) conditional(s32[]{:T(128)} %convert_element_type.70, (f32[1,8,128]{2,1,0:T(8,128)S(1)}, f32[1,8,128]{2,1,0:T(8,128)S(1)}, f32[1,8,128,128]{3,2,1,0:T(8,128)S(1)}) %tuple.75, (s32[2048]{0:T(1024)S(1)}, s32[256]{0:T(256)S(1)}, ...), branch_computations={%region_4.0_spmd, %region_5.7_spmd} | conditional | flops 1097337856 | bytes 30746172 | solution.py:103
  281.5 2.3 fusion.12
  291.7 5.9 %conditional.4 = ((f32[1,8,128]{2,1,0:T(8,128)S(1)}, f32[1,8,128]{2,1,0:T(8,128)S(1)}, f32[1,8,128,128]{3,2,1,0:T(8,128)S(1)})) conditional(s32[]{:T(128)} %convert_element_type.69, (f32[1,8,128]{2,1,0:T(8,128)S(1)}, f32[1,8,128]{2,1,0:T(8,128)S(1)}, f32[1,8,128,128]{3,2,1,0:T(8,128)S(1)}) %tuple.73, (s32[2048]{0:T(1024)S(1)}, s32[256]{0:T(256)S(1)}, ...), branch_computations={%region_8.8_spmd, %region_9.11_spmd} | conditional | flops 1097337856 | bytes 30746172 | solution.py:103
  293.4 2.3 fusion.35
  297.5 5.9 %conditional.5 = ((f32[1,8,128]{2,1,0:T(8,128)S(1)}, f32[1,8,128]{2,1,0:T(8,128)S(1)}, f32[1,8,128,128]{3,2,1,0:T(8,128)S(1)})) conditional(s32[]{:T(128)} %convert_element_type.70, (f32[1,8,128]{2,1,0:T(8,128)S(1)}, f32[1,8,128]{2,1,0:T(8,128)S(1)}, f32[1,8,128,128]{3,2,1,0:T(8,128)S(1)}) %tuple.75, (s32[2048]{0:T(1024)S(1)}, s32[256]{0:T(256)S(1)}, ...), branch_computations={%region_4.0_spmd, %region_5.7_spmd} | conditional | flops 1097337856 | bytes 30746172 | solution.py:103
  299.3 2.3 fusion.12
  309.5 5.9 %conditional.4 = ((f32[1,8,128]{2,1,0:T(8,128)S(1)}, f32[1,8,128]{2,1,0:T(8,128)S(1)}, f32[1,8,128,128]{3,2,1,0:T(8,128)S(1)})) conditional(s32[]{:T(128)} %convert_element_type.69, (f32[1,8,128]{2,1,0:T(8,128)S(1)}, f32[1,8,128]{2,1,0:T(8,128)S(1)}, f32[1,8,128,128]{3,2,1,0:T(8,128)S(1)}) %tuple.73, (s32[2048]{0:T(1024)S(1)}, s32[256]{0:T(256)S(1)}, ...), branch_computations={%region_8.8_spmd, %region_9.11_spmd} | conditional | flops 1097337856 | bytes 30746172 | solution.py:103
  311.3 2.3 fusion.35
  315.4 5.9 %conditional.5 = ((f32[1,8,128]{2,1,0:T(8,128)S(1)}, f32[1,8,128]{2,1,0:T(8,128)S(1)}, f32[1,8,128,128]{3,2,1,0:T(8,128)S(1)})) conditional(s32[]{:T(128)} %convert_element_type.70, (f32[1,8,128]{2,1,0:T(8,128)S(1)}, f32[1,8,128]{2,1,0:T(8,128)S(1)}, f32[1,8,128,128]{3,2,1,0:T(8,128)S(1)}) %tuple.75, (s32[2048]{0:T(1024)S(1)}, s32[256]{0:T(256)S(1)}, ...), branch_computations={%region_4.0_spmd, %region_5.7_spmd} | conditional | flops 1097337856 | bytes 30746172 | solution.py:103
  317.1 2.3 fusion.12
  327.3 5.9 %conditional.4 = ((f32[1,8,128]{2,1,0:T(8,128)S(1)}, f32[1,8,128]{2,1,0:T(8,128)S(1)}, f32[1,8,128,128]{3,2,1,0:T(8,128)S(1)})) conditional(s32[]{:T(128)} %convert_element_type.69, (f32[1,8,128]{2,1,0:T(8,128)S(1)}, f32[1,8,128]{2,1,0:T(8,128)S(1)}, f32[1,8,128,128]{3,2,1,0:T(8,128)S(1)}) %tuple.73, (s32[2048]{0:T(1024)S(1)}, s32[256]{0:T(256)S(1)}, ...), branch_computations={%region_8.8_spmd, %region_9.11_spmd} | conditional | flops 1097337856 | bytes 30746172 | solution.py:103
  329.1 2.3 fusion.35
  333.2 5.9 %conditional.5 = ((f32[1,8,128]{2,1,0:T(8,128)S(1)}, f32[1,8,128]{2,1,0:T(8,128)S(1)}, f32[1,8,128,128]{3,2,1,0:T(8,128)S(1)})) conditional(s32[]{:T(128)} %convert_element_type.70, (f32[1,8,128]{2,1,0:T(8,128)S(1)}, f32[1,8,128]{2,1,0:T(8,128)S(1)}, f32[1,8,128,128]{3,2,1,0:T(8,128)S(1)}) %tuple.75, (s32[2048]{0:T(1024)S(1)}, s32[256]{0:T(256)S(1)}, ...), branch_computations={%region_4.0_spmd, %region_5.7_spmd} | conditional | flops 1097337856 | bytes 30746172 | solution.py:103
  345.2 5.9 %conditional.4 = ((f32[1,8,128]{2,1,0:T(8,128)S(1)}, f32[1,8,128]{2,1,0:T(8,128)S(1)}, f32[1,8,128,128]{3,2,1,0:T(8,128)S(1)})) conditional(s32[]{:T(128)} %convert_element_type.69, (f32[1,8,128]{2,1,0:T(8,128)S(1)}, f32[1,8,128]{2,1,0:T(8,128)S(1)}, f32[1,8,128,128]{3,2,1,0:T(8,128)S(1)}) %tuple.73, (s32[2048]{0:T(1024)S(1)}, s32[256]{0:T(256)S(1)}, ...), branch_computations={%region_8.8_spmd, %region_9.11_spmd} | conditional | flops 1097337856 | bytes 30746172 | solution.py:103
  351.0 5.9 %conditional.5 = ((f32[1,8,128]{2,1,0:T(8,128)S(1)}, f32[1,8,128]{2,1,0:T(8,128)S(1)}, f32[1,8,128,128]{3,2,1,0:T(8,128)S(1)})) conditional(s32[]{:T(128)} %convert_element_type.70, (f32[1,8,128]{2,1,0:T(8,128)S(1)}, f32[1,8,128]{2,1,0:T(8,128)S(1)}, f32[1,8,128,128]{3,2,1,0:T(8,128)S(1)}) %tuple.75, (s32[2048]{0:T(1024)S(1)}, s32[256]{0:T(256)S(1)}, ...), branch_computations={%region_4.0_spmd, %region_5.7_spmd} | conditional | flops 1097337856 | bytes 30746172 | solution.py:103
  352.8 2.3 fusion.12
  363.0 5.9 %conditional.4 = ((f32[1,8,128]{2,1,0:T(8,128)S(1)}, f32[1,8,128]{2,1,0:T(8,128)S(1)}, f32[1,8,128,128]{3,2,1,0:T(8,128)S(1)})) conditional(s32[]{:T(128)} %convert_element_type.69, (f32[1,8,128]{2,1,0:T(8,128)S(1)}, f32[1,8,128]{2,1,0:T(8,128)S(1)}, f32[1,8,128,128]{3,2,1,0:T(8,128)S(1)}) %tuple.73, (s32[2048]{0:T(1024)S(1)}, s32[256]{0:T(256)S(1)}, ...), branch_computations={%region_8.8_spmd, %region_9.11_spmd} | conditional | flops 1097337856 | bytes 30746172 | solution.py:103
  368.9 5.9 %conditional.5 = ((f32[1,8,128]{2,1,0:T(8,128)S(1)}, f32[1,8,128]{2,1,0:T(8,128)S(1)}, f32[1,8,128,128]{3,2,1,0:T(8,128)S(1)})) conditional(s32[]{:T(128)} %convert_element_type.70, (f32[1,8,128]{2,1,0:T(8,128)S(1)}, f32[1,8,128]{2,1,0:T(8,128)S(1)}, f32[1,8,128,128]{3,2,1,0:T(8,128)S(1)}) %tuple.75, (s32[2048]{0:T(1024)S(1)}, s32[256]{0:T(256)S(1)}, ...), branch_computations={%region_4.0_spmd, %region_5.7_spmd} | conditional | flops 1097337856 | bytes 30746172 | solution.py:103
  380.8 5.9 %conditional.4 = ((f32[1,8,128]{2,1,0:T(8,128)S(1)}, f32[1,8,128]{2,1,0:T(8,128)S(1)}, f32[1,8,128,128]{3,2,1,0:T(8,128)S(1)})) conditional(s32[]{:T(128)} %convert_element_type.69, (f32[1,8,128]{2,1,0:T(8,128)S(1)}, f32[1,8,128]{2,1,0:T(8,128)S(1)}, f32[1,8,128,128]{3,2,1,0:T(8,128)S(1)}) %tuple.73, (s32[2048]{0:T(1024)S(1)}, s32[256]{0:T(256)S(1)}, ...), branch_computations={%region_8.8_spmd, %region_9.11_spmd} | conditional | flops 1097337856 | bytes 30746172 | solution.py:103
  386.7 5.9 %conditional.5 = ((f32[1,8,128]{2,1,0:T(8,128)S(1)}, f32[1,8,128]{2,1,0:T(8,128)S(1)}, f32[1,8,128,128]{3,2,1,0:T(8,128)S(1)})) conditional(s32[]{:T(128)} %convert_element_type.70, (f32[1,8,128]{2,1,0:T(8,128)S(1)}, f32[1,8,128]{2,1,0:T(8,128)S(1)}, f32[1,8,128,128]{3,2,1,0:T(8,128)S(1)}) %tuple.75, (s32[2048]{0:T(1024)S(1)}, s32[256]{0:T(256)S(1)}, ...), branch_computations={%region_4.0_spmd, %region_5.7_spmd} | conditional | flops 1097337856 | bytes 30746172 | solution.py:103
  388.5 2.3 fusion.12
  398.7 5.9 %conditional.4 = ((f32[1,8,128]{2,1,0:T(8,128)S(1)}, f32[1,8,128]{2,1,0:T(8,128)S(1)}, f32[1,8,128,128]{3,2,1,0:T(8,128)S(1)})) conditional(s32[]{:T(128)} %convert_element_type.69, (f32[1,8,128]{2,1,0:T(8,128)S(1)}, f32[1,8,128]{2,1,0:T(8,128)S(1)}, f32[1,8,128,128]{3,2,1,0:T(8,128)S(1)}) %tuple.73, (s32[2048]{0:T(1024)S(1)}, s32[256]{0:T(256)S(1)}, ...), branch_computations={%region_8.8_spmd, %region_9.11_spmd} | conditional | flops 1097337856 | bytes 30746172 | solution.py:103
  404.5 5.9 %conditional.5 = ((f32[1,8,128]{2,1,0:T(8,128)S(1)}, f32[1,8,128]{2,1,0:T(8,128)S(1)}, f32[1,8,128,128]{3,2,1,0:T(8,128)S(1)})) conditional(s32[]{:T(128)} %convert_element_type.70, (f32[1,8,128]{2,1,0:T(8,128)S(1)}, f32[1,8,128]{2,1,0:T(8,128)S(1)}, f32[1,8,128,128]{3,2,1,0:T(8,128)S(1)}) %tuple.75, (s32[2048]{0:T(1024)S(1)}, s32[256]{0:T(256)S(1)}, ...), branch_computations={%region_4.0_spmd, %region_5.7_spmd} | conditional | flops 1097337856 | bytes 30746172 | solution.py:103
  411.4 19.8 %all_to_all.65 = bf16[4,64,1024]{2,1,0:T(8,128)(2,1)S(1)} all-to-all(bf16[4,64,1024]{2,1,0:T(8,128)(2,1)S(1)} %convert_element_type.47), channel_id=1, replica_groups=mesh['blk'=64,'head'=4] {'head'}, dimensions={0} | all-to-all | bytes 1048576 | tf_op jit(solution)/shard_map/all_to_all | solution.py:166
  (248 shorter events, 112.9 us)
Async XLA Ops:
  7.4 0.8 copy-start
  8.8 16.7 %all-to-all-start.1 = ((bf16[64,4,128]{2,0,1:T(8,128)(2,1)}), bf16[64,4,128]{2,0,1:T(8,128)(2,1)S(1)}, u32[]{:S(2)}, u32[]{:S(2)}) async-start(bf16[64,4,128]{2,0,1:T(8,128)(2,1)} %copy_bitcast_fusion), calls=%async_computation.1 | async-start | bytes 131072 | tf_op jit(solution)/shard_map/all_to_all | solution.py:148
  17.3 248.6 %all-reduce.3.cloned.1.call-start = ((), (), s32[]{:S(2)}) async-start(), calls=%async_computation.6 | async-start | bytes 131072
  18.2 0.6 copy-start.4
  18.8 248.7 %all-gather.5.cloned.1.call-start = ((), (), s32[]{:S(2)}) async-start(), calls=%async_computation.5 | async-start | bytes 4259840 | tf_op jit(solution)/shard_map/all_gather | solution.py:161
  25.5 0.6 copy-start.3
  26.2 241.4 %all-gather.3.cloned.1.call-start = ((), (), s32[]{:S(2)}) async-start(), calls=%async_computation.4 | async-start | bytes 4259840 | tf_op jit(solution)/shard_map/all_gather | solution.py:160
  43.4 223.9 %all-to-all-start.2 = ((bf16[64,4,1024]{2,0,1:T(8,128)(2,1)}), bf16[64,4,1024]{2,0,1:T(8,128)(2,1)S(1)}, u32[]{:S(2)}, u32[]{:S(2)}) async-start(bf16[64,4,1024]{2,0,1:T(8,128)(2,1)} %copy.33), calls=%async_computation.2 | async-start | bytes 1048576 | tf_op jit(solution)/shard_map/all_to_all | solution.py:146
  273.8 1.8 copy-start.1
  279.7 1.8 copy-start.2
  291.7 1.8 copy-start.1
  297.5 1.8 copy-start.2
  309.5 1.8 copy-start.1
  315.4 1.8 copy-start.2
  327.3 1.8 copy-start.1
  333.2 1.8 copy-start.2
  345.2 1.8 copy-start.1
  351.0 1.8 copy-start.2
  363.0 1.8 copy-start.1
  368.9 1.8 copy-start.2
  380.9 1.8 copy-start.1
  386.7 1.8 copy-start.2
  398.7 1.8 copy-start.1
  404.6 1.8 copy-start.2
Sparse Core Ops, SparseCore 0:
  23.6 242.2 all-reduce.2
Sparse Core Ops, SparseCore 1:
  26.2 107.0 all-gather.4
  135.0 106.0 all-gather.2
where the time goes:
time: 441 us; the launch traced here: 440 us
  waiting for transfers between devices  226 us (51%)
  matrix products  59.2 us (13%)
  other arithmetic  49 us (11%)
  blocking collectives  31.1 us (7%)
  local copies, waits for them, and re-layouts  25.6 us (6%)
  loops' own time  22 us (5%)
  between operations  15 us (3%)
  starting transfers between devices  12 us (3%)
    unnamed x4, waiting for transfers between devices  219 us
    dot_general x16, matrix products, attend(): jnp.einsum('grqk,kgd->grqd', weights.astype(jnp.bfloat16), value_rows, pr...  37.4 us
    reduce_sum x16, other arithmetic, attend(): total = total * factor + jnp.sum(weights, axis=3)  27.4 us
    dot_general x16, matrix products, attend(): jnp.einsum('qgrd,kgd->grqk', query_rows, key_rows, preferred_element_type...  21.7 us
    another operation x1, loops' own time, fold(): return lax.fori_loop(0, count // step_rows, inner, state)  20.7 us
    all_to_all x1, blocking collectives, body(): lax.all_to_all(mixed, 'head', split_axis=0, concat_axis=1, tiled=True)  19.8 us
    dynamic_slice x8, local copies, waits for them, and re-layouts, inner(): value_block = lax.dynamic_slice_in_dim(value_part, begin, step_rows, 0)  16.5 us
    all_to_all x1, blocking collectives, body(): lax.all_to_all(k_rot, 'head', split_axis=1, concat_axis=0, tiled=True)  11.2 us
  transfers between devices with their start and end apart: 5, of which 2 were waited for; matrix products, arithmetic and copies ran while one was open for 2% of the time, Pallas kernels for 0%

commit v1 on v0

v1 whole, which is shorter than its diff:
```python
import functools
import math

import jax
import jax.numpy as jnp
import numpy as np
from jax import lax
from jax.experimental import pallas as pl
from jax.experimental.pallas import tpu as pltpu
from jax.sharding import PartitionSpec as P

QHEADS = 32
KVHEADS = 4
HEAD_DIM = 128


def rope_table(size):
    entries = []
    for number in range(size // 2):
        inverse = 1.0 / 500000.0 ** (2.0 * number / size)
        wavelength = 2.0 * math.pi / inverse
        if wavelength < 2048.0:
            entries.append(inverse)
        elif wavelength > 8192.0:
            entries.append(inverse / 8.0)
        else:
            smooth = (8192.0 / wavelength - 1.0) / 3.0
            entries.append((1.0 - smooth) * inverse / 8.0 + smooth * inverse)
    return np.array(entries, dtype=np.float32)


F32 = jnp.float32
BF16 = jnp.bfloat16
MESH = pl.DeviceIdType.MESH
SCALE = math.log2(math.e) * HEAD_DIM ** (-0.5)
SAFE = 100.0
NORM_CAP = (SAFE / SCALE) ** 2
PART = 64
SPAN = 128
GROUP = QHEADS // KVHEADS
COLS = GROUP * SPAN
EXTRA = 16
ROWS = 4 * SPAN + EXTRA
HALF = 256
PIECE = 2 * PART + EXTRA
NBLK = 8
CHUNK = 512
TAIL = 256


def turn(x, cosine, sine):
    return x * cosine + pltpu.roll(x, HEAD_DIM // 2, 1) * sine


def fused(
    shifted,
    q_hbm, k_hbm, v_hbm, pos_hbm, table_hbm,
    out_ref, ok_ref,
    q_ref, k_ref, v_ref, pos_ref, table_ref,
    kv, piece_out, piece_in, q_out, q_in, qc, ka, kc, va, vc, flags,
    acc_lo, acc_hi, top_lo, top_hi, o_out,
    in_sem, p_ss, p_rs, q_ss, q_rs, o_ss, o_rs, rs, rsc, ss_core, ss1, ss2, ss_z,
):
    blk = lax.axis_index("blk")
    hd = lax.axis_index("head")
    core = blk % 2
    zz = (blk // 2) % 2
    yy = (blk // 4) % 4
    xx = blk // 16

    def bid(x, y, z, c):
        return (((x + 8) % 4) * 4 + (y + 8) % 4) * 4 + z * 2 + c

    xp, xm = bid(xx + 1, yy, zz, core), bid(xx + 3, yy, zz, core)
    yp, ym = bid(xx, yy + 1, zz, core), bid(xx, yy + 3, zz, core)
    zn = bid(xx, yy, 1 - zz, core)
    cn = bid(xx, yy, zz, 1 - core)

    barrier = pltpu.get_barrier_semaphore()
    for peer in (xp, xm, yp, ym, zn, cn):
        pl.semaphore_signal(barrier, inc=1, device_id=(peer, hd), device_id_type=MESH)
    for d in (1, 2, 3):
        pl.semaphore_signal(barrier, inc=1, device_id=(blk, (hd + d) % 4), device_id_type=MESH)

    loads = [
        pltpu.make_async_copy(a, b, in_sem.at[n])
        for n, (a, b) in enumerate((
            (pos_hbm, pos_ref), (table_hbm, table_ref), (k_hbm, k_ref), (v_hbm, v_ref), (q_hbm, q_ref)))
    ]
    for load in loads:
        load.start()

    ones_m = jnp.ones((HEAD_DIM, HEAD_DIM), BF16)

    def norms(ref, count):
        best = jnp.zeros((PART, HEAD_DIM), F32)
        for g in range(count):
            x = ref[:, g * HEAD_DIM : (g + 1) * HEAD_DIM].astype(F32)
            best = jnp.maximum(best, jnp.dot((x * x).astype(BF16), ones_m, preferred_element_type=F32))
        return jnp.max(best, axis=0, keepdims=True) * 1.03

    row16 = lax.broadcasted_iota(jnp.int32, (EXTRA, HEAD_DIM), 0)

    def extras(span, qn, kn):
        return jnp.where(row16 < 4, span, jnp.where(row16 < 8, qn, kn)).astype(BF16)

    loads[0].wait()
    loads[1].wait()
    place = pos_ref[0]
    angles = (place + lax.broadcasted_iota(jnp.int32, (PART, HEAD_DIM), 0)).astype(F32) * table_ref[0:1]
    cosine = jnp.cos(angles)
    sine = jnp.sin(angles)
    sine = jnp.where(lax.broadcasted_iota(jnp.int32, (PART, HEAD_DIM), 1) < HEAD_DIM // 2, -sine, sine)
    for load in loads[2:]:
        load.wait()
    span = jnp.full((1, HEAD_DIM), place // SPAN, jnp.int32).astype(F32)
    ext = extras(span, norms(q_ref, QHEADS), norms(k_ref, KVHEADS))
    for g in range(KVHEADS):
        cols = slice(g * HEAD_DIM, (g + 1) * HEAD_DIM)
        piece_out[g, 0:PART] = turn(k_ref[:, cols].astype(F32), cosine, sine).astype(BF16)
        piece_out[g, PART : 2 * PART] = v_ref[:, cols]
        piece_out[g, 2 * PART : PIECE] = ext
    pl.semaphore_wait(barrier, 9)

    def piece_copy(d):
        tgt = (hd + d) % 4
        return pltpu.make_async_remote_copy(
            src_ref=piece_out.at[tgt], dst_ref=piece_in.at[hd],
            send_sem=p_ss.at[d - 1], recv_sem=p_rs.at[d - 1],
            device_id=(blk, tgt), device_id_type=MESH)

    for d in (2, 1, 3):
        piece_copy(d).start()
    piece_in[hd] = piece_out[hd]

    for g in range(KVHEADS):
        for i in range(GROUP):
            n = g * GROUP + i
            x = q_ref[:, n * HEAD_DIM : (n + 1) * HEAD_DIM].astype(F32)
            q_out[g, i * PART : (i + 1) * PART] = turn(x, cosine, sine).astype(BF16)

    def q_copy(d):
        tgt = (hd + d) % 4
        return pltpu.make_async_remote_copy(
            src_ref=q_out.at[tgt], dst_ref=q_in.at[hd],
            send_sem=q_ss.at[d - 1], recv_sem=q_rs.at[d - 1],
            device_id=(blk, tgt), device_id_type=MESH)

    def recv_piece(d):
        src = (hd + 4 - d) % 4
        pltpu.make_async_remote_copy(
            src_ref=piece_out.at[src], dst_ref=piece_in.at[src],
            send_sem=p_ss.at[d - 1], recv_sem=p_rs.at[d - 1],
            device_id=(blk, src), device_id_type=MESH).wait_recv()

    def recv_q(d):
        src = (hd + 4 - d) % 4
        pltpu.make_async_remote_copy(
            src_ref=q_out.at[src], dst_ref=q_in.at[src],
            send_sem=q_ss.at[d - 1], recv_sem=q_rs.at[d - 1],
            device_id=(blk, src), device_id_type=MESH).wait_recv()

    for d in (1, 2, 3):
        recv_piece(d)

    e = [piece_in[h, 2 * PART : PIECE].astype(F32) for h in range(4)]
    s0, s1 = e[0][0:1], e[2][0:1]
    low_first = s0 < s1
    mine = jnp.minimum(s0, s1)
    qn = jnp.maximum(jnp.maximum(e[0][4:5], e[1][4:5]), jnp.maximum(e[2][4:5], e[3][4:5]))
    kn = jnp.maximum(jnp.maximum(e[0][8:9], e[1][8:9]), jnp.maximum(e[2][8:9], e[3][8:9]))
    pick = jnp.broadcast_to(low_first, (SPAN, HEAD_DIM))

    def spans(load):
        first = jnp.concatenate([load(0), load(1)], axis=0).astype(F32)
        second = jnp.concatenate([load(2), load(3)], axis=0).astype(F32)
        return first, second

    k0, k1 = spans(lambda h: piece_in[h, 0:PART])
    v0, v1 = spans(lambda h: piece_in[h, PART : 2 * PART])
    v0, v1 = v0.T, v1.T
    kv[blk, 0:SPAN] = jnp.where(pick, k0, k1).astype(BF16)
    kv[blk, SPAN : 2 * SPAN] = jnp.where(pick, k1, k0).astype(BF16)
    kv[blk, 2 * SPAN : 3 * SPAN] = jnp.where(pick, v0, v1).astype(BF16)
    kv[blk, 3 * SPAN : 4 * SPAN] = jnp.where(pick, v1, v0).astype(BF16)
    kv[blk, 4 * SPAN : ROWS] = extras(mine, qn, kn)

    def slot(t, p, i, c):
        x = xx + (1 - t) * i + t * p
        y = yy + (1 - t) * p + t * i
        z = zz + t - 2 * zz * t
        return bid(x, y, z, c)

    def copy(t, p, i, lo, n, dev, ss, sem):
        b = slot(t, p, i, core)
        ref = kv.at[b, pl.ds(lo, n)]
        return pltpu.make_async_remote_copy(
            src_ref=ref, dst_ref=ref, send_sem=ss, recv_sem=sem,
            device_id=(dev, hd), device_id_type=MESH)

    def rid(t, p, i):
        return t * 16 + p * 4 + i

    def near(t, axis, d):
        a = t if axis == 0 else 1 - t
        return bid(xx + (1 - a) * d, yy + a * d, zz, core)

    def core_copy(t, p, i):
        return copy(t, p, i, 0, ROWS, cn, ss_core.at[rid(t, p, i)], rsc.at[rid(t, p, i)])

    def core_recv(t, p, i):
        b = slot(t, p, i, 1 - core)
        ref = kv.at[b]
        pltpu.make_async_remote_copy(
            src_ref=ref, dst_ref=ref, send_sem=ss_core.at[rid(t, p, i)],
            recv_sem=rsc.at[rid(t, p, i)], device_id=(cn, hd), device_id_type=MESH).wait_recv()

    def z_copy():
        return pltpu.make_async_remote_copy(
            src_ref=kv.at[blk], dst_ref=kv.at[blk], send_sem=ss_z.at[0],
            recv_sem=rs.at[rid(1, 0, 0), 0], device_id=(zn, hd), device_id_type=MESH)

    def first_copy(t, d):
        return copy(t, 0, 0, 0, ROWS, near(t, 0, d), ss1.at[t * 4 + (0 if d == 1 else 1)],
                    rs.at[rid(t, 0, 3 if d == 1 else 1), 0])

    def first_forward(t, d):
        lo, n = (0, HALF) if d == 1 else (HALF, ROWS - HALF)
        return copy(t, 0, 3 if d == 1 else 1, lo, n, near(t, 0, d),
                    ss1.at[t * 4 + (2 if d == 1 else 3)], rs.at[rid(t, 0, 2), 0 if d == 1 else 1])

    def second_copy(t, i, d):
        return copy(t, 0, i, 0, ROWS, near(t, 1, d), ss2.at[t * 16 + i * 4 + (0 if d == 1 else 1)],
                    rs.at[rid(t, 3 if d == 1 else 1, i), 0])

    def second_forward(t, i, d):
        lo, n = (0, HALF) if d == 1 else (HALF, ROWS - HALF)
        return copy(t, 3 if d == 1 else 1, i, lo, n, near(t, 1, d),
                    ss2.at[t * 16 + i * 4 + (2 if d == 1 else 3)],
                    rs.at[rid(t, 2, i), 0 if d == 1 else 1])

    def recv_full(t, p, i):
        copy(t, p, i, 0, ROWS, cn, ss_core.at[rid(t, p, i)], rs.at[rid(t, p, i), 0]).wait_recv()

    def recv_halves(t, p, i):
        for part, (lo, n) in enumerate(((0, HALF), (HALF, ROWS - HALF))):
            copy(t, p, i, lo, n, cn, ss_core.at[rid(t, p, i)], rs.at[rid(t, p, i), part]).wait_recv()

    def second(t, i):
        for d in (1, -1):
            second_copy(t, i, d).start()

    def arrive(t, p, i):
        if p == 2:
            recv_halves(t, p, i)
        else:
            recv_full(t, p, i)
            second_forward(t, i, 1 if p == 3 else -1).start()
        core_copy(t, p, i).start()

    def spread(t, i):
        second(t, i)
        core_copy(t, 0, i).start()

    z_copy().start()
    for d in (1, -1):
        first_copy(0, d).start()
    spread(0, 0)
    recv_full(1, 0, 0)
    for d in (1, -1):
        first_copy(1, d).start()
    spread(1, 0)
    for d in (2, 1, 3):
        q_copy(d).start()
    q_in[hd] = q_out[hd]
    for t in (0, 1):
        for d in (1, -1):
            recv_full(t, 0, 3 if d == 1 else 1)
            first_forward(t, d).start()
            spread(t, 3 if d == 1 else 1)
    for t in (0, 1):
        recv_halves(t, 0, 2)
        spread(t, 2)

    acc_lo[...] = jnp.zeros_like(acc_lo)
    acc_hi[...] = jnp.zeros_like(acc_hi)
    for s in range(2):
        va[s, SPAN : SPAN + EXTRA] = jnp.ones((EXTRA, NBLK * SPAN), BF16)

    def prepare_queries():
        for d in (1, 2, 3):
            recv_q(d)
        for i in range(GROUP):
            a, b = spans(lambda h: q_in[h, i * PART : (i + 1) * PART])
            a, b = a.T, b.T
            qc[0:SPAN, i * SPAN : (i + 1) * SPAN] = jnp.where(pick, a, b).astype(BF16)
            qc[SPAN:, i * SPAN : (i + 1) * SPAN] = jnp.where(pick, b, a).astype(BF16)

    def diagonal():
        key_row = lax.broadcasted_iota(jnp.int32, (SPAN, COLS), 0)
        token = lax.broadcasted_iota(jnp.int32, (SPAN, COLS), 1) % SPAN
        seen = key_row <= token
        for n, (acc, top) in enumerate(((acc_lo, top_lo), (acc_hi, top_hi))):
            keys = kv[blk, n * SPAN : (n + 1) * SPAN]
            vals = kv[blk, (2 + n) * SPAN : (3 + n) * SPAN]
            scores = jnp.dot(keys, qc[n * SPAN : (n + 1) * SPAN], preferred_element_type=F32) * SCALE
            if shifted:
                best = jnp.max(jnp.where(seen, scores, -1e30), axis=0, keepdims=True)
                top[...] = jnp.broadcast_to(best, (8, COLS))
                scores = scores - best
            weights = jnp.where(seen, jnp.exp2(scores), 0.0).astype(BF16)
            vals = jnp.concatenate([vals, jnp.ones((EXTRA, SPAN), BF16)], axis=0)
            acc[...] += jnp.dot(vals, weights, preferred_element_type=F32)[0 : SPAN + 8]

    def gather_stage(t, p, s):
        for i in range(4):
            core_recv(t, p, i)
        for c in range(2):
            for i in range(4):
                n = c * 4 + i
                keys = slice(n * SPAN, (n + 1) * SPAN)
                b = slot(t, p, i, core if c == 0 else 1 - core)
                j = kv[b, 4 * SPAN : ROWS].astype(F32)[0:1]
                below = jnp.where(j < mine, 1.0, 0.0)
                above = jnp.where(j > mine, 1.0, 0.0)
                lower = jnp.broadcast_to(below, (SPAN, HEAD_DIM)).astype(BF16)
                upper = jnp.broadcast_to(above, (SPAN, HEAD_DIM)).astype(BF16)
                k_low = kv[b, 0:SPAN]
                v_low = kv[b, 2 * SPAN : 3 * SPAN]
                ka[s, keys] = k_low
                va[s, 0:SPAN, keys] = v_low
                kc[s, keys, 0:SPAN] = k_low * lower
                kc[s, keys, SPAN:] = kv[b, SPAN : 2 * SPAN] * upper
                vc[s, 0:SPAN, keys] = v_low * lower
                vc[s, SPAN : 2 * SPAN, keys] = kv[b, 3 * SPAN : 4 * SPAN] * upper
                vc[s, 2 * SPAN :, keys] = jnp.where(row16 < 8, below, above).astype(BF16)
                if shifted:
                    flags[s, n] = jnp.where(row16 < 8, below, above)

    def add_both(both, cols, scale_lo, scale_hi):
        acc_lo[0:SPAN, cols] = acc_lo[0:SPAN, cols] * scale_lo + both[0:SPAN]
        acc_lo[SPAN:, cols] = acc_lo[SPAN:, cols] * scale_lo + both[2 * SPAN : 2 * SPAN + 8]
        acc_hi[0:SPAN, cols] = acc_hi[0:SPAN, cols] * scale_hi + both[SPAN : 2 * SPAN]
        acc_hi[SPAN:, cols] = acc_hi[SPAN:, cols] * scale_hi + both[2 * SPAN + 8 :]

    def work_shifted(s, cols):
        width = cols.stop - cols.start

        @pl.loop(0, NBLK)
        def _(n):
            keys = pl.ds(pl.multiple_of(n * SPAN, SPAN), SPAN)
            lower = jnp.concatenate([flags[s, n, 0:1]] * (width // HEAD_DIM), axis=1) > 0.5
            upper = jnp.concatenate([flags[s, n, 8:9]] * (width // HEAD_DIM), axis=1) > 0.5
            scores = jnp.dot(ka[s, keys], qc[SPAN:, cols], preferred_element_type=F32) * SCALE
            old = top_hi[0:1, cols]
            new = jnp.maximum(old, jnp.max(scores, axis=0, keepdims=True))
            weights = jnp.exp2(scores - new).astype(BF16)
            part = jnp.dot(va[s, :, keys], weights, preferred_element_type=F32)[0 : SPAN + 8]
            acc_hi[:, cols] = acc_hi[:, cols] * jnp.exp2(old - new) + part
            old_hi, old_lo = new, top_lo[0:1, cols]
            scores = jnp.dot(kc[s, keys], qc[:, cols], preferred_element_type=F32) * SCALE
            best = jnp.max(scores, axis=0, keepdims=True)
            new_lo = jnp.where(lower, jnp.maximum(old_lo, best), old_lo)
            new_hi = jnp.where(upper, jnp.maximum(old_hi, best), old_hi)
            shift = jnp.where(lower, new_lo, new_hi)
            weights = jnp.where(lower | upper, jnp.exp2(scores - shift), 0.0).astype(BF16)
            both = jnp.dot(vc[s, :, keys], weights, preferred_element_type=F32)
            add_both(both, cols, jnp.exp2(old_lo - new_lo), jnp.exp2(old_hi - new_hi))
            top_lo[:, cols] = jnp.broadcast_to(new_lo, (8, width))
            top_hi[:, cols] = jnp.broadcast_to(new_hi, (8, width))

    def work(s, cols):
        if shifted:
            work_shifted(s, cols)
            return
        scores = jnp.dot(ka[s], qc[SPAN:, cols], preferred_element_type=F32)
        weights = jnp.exp2(scores * SCALE).astype(BF16)
        acc_hi[:, cols] += jnp.dot(va[s], weights, preferred_element_type=F32)[0 : SPAN + 8]
        scores = jnp.dot(kc[s], qc[:, cols], preferred_element_type=F32)
        weights = jnp.exp2(scores * SCALE).astype(BF16)
        both = jnp.dot(vc[s], weights, preferred_element_type=F32)
        acc_lo[0:SPAN, cols] += both[0:SPAN]
        acc_lo[SPAN:, cols] += both[2 * SPAN : 2 * SPAN + 8]
        acc_hi[0:SPAN, cols] += both[SPAN : 2 * SPAN]
        acc_hi[SPAN:, cols] += both[2 * SPAN + 8 :]

    halves = [slice(c * CHUNK, (c + 1) * CHUNK) for c in range(COLS // CHUNK)]
    tails = [slice(c * TAIL, (c + 1) * TAIL) for c in range(COLS // TAIL)]

    def stage(t, p, s, between=()):
        gather_stage(t, p, s)
        between = list(between)
        for n, cols in enumerate(halves):
            work(s, cols)
            share = -(-len(between) // (len(halves) - n))
            for task in between[:share]:
                arrive(*task)
            between = between[share:]

    def o_copy(d, c, src):
        tgt = (hd + d) % 4
        start = pl.multiple_of(src * COLS + c * TAIL, TAIL)
        return pltpu.make_async_remote_copy(
            src_ref=o_out.at[tgt, :, pl.ds(c * TAIL, TAIL)], dst_ref=out_ref.at[:, pl.ds(start, TAIL)],
            send_sem=o_ss.at[d - 1, c], recv_sem=o_rs.at[d - 1, c],
            device_id=(blk, tgt), device_id_type=MESH)

    def own_copy(c):
        start = pl.multiple_of(hd * COLS + c * TAIL, TAIL)
        return pltpu.make_async_copy(
            o_out.at[hd, :, pl.ds(c * TAIL, TAIL)], out_ref.at[:, pl.ds(start, TAIL)], o_ss.at[3, c])

    def finish(c):
        for i in range(c * TAIL // SPAN, (c + 1) * TAIL // SPAN):
            cols = slice(i * SPAN, (i + 1) * SPAN)
            low = (acc_lo[0:SPAN, cols] * (1.0 / acc_lo[SPAN : SPAN + 1, cols])).T
            high = (acc_hi[0:SPAN, cols] * (1.0 / acc_hi[SPAN : SPAN + 1, cols])).T
            first = jnp.where(pick, low, high).astype(BF16)
            second_rows = jnp.where(pick, high, low).astype(BF16)
            o_out[0, :, cols] = first[:PART]
            o_out[1, :, cols] = first[PART:]
            o_out[2, :, cols] = second_rows[:PART]
            o_out[3, :, cols] = second_rows[PART:]
        for d in (2, 1, 3):
            o_copy(d, c, hd).start()
        own_copy(c).start()

    def ring(t, p):
        return [(t, p, i) for i in (0, 3, 1, 2)]

    def take(tasks):
        for task in tasks:
            arrive(*task)

    prepare_queries()
    diagonal()
    stage(0, 0, 0)
    take(ring(0, 3) + ring(0, 1) + ring(1, 3) + ring(1, 1))
    stage(1, 0, 1)
    stage(0, 3, 0)
    stage(1, 3, 1)
    take(ring(0, 2) + ring(1, 2))
    stage(0, 1, 0)
    stage(1, 1, 1)
    gather_stage(0, 2, 0)
    gather_stage(1, 2, 1)
    for c, cols in enumerate(tails):
        work(0, cols)
        work(1, cols)
        finish(c)
    def worst(b, carry):
        x = kv[b, 4 * SPAN : ROWS].astype(F32)
        return jnp.maximum(carry, x)

    top = lax.fori_loop(0, 64, worst, jnp.zeros((EXTRA, HEAD_DIM), F32))
    ok_ref[0, 0] = jnp.max(jnp.where(top[4:5] * top[8:9] <= NORM_CAP, 1, 0))

    for d in (1, 2, 3):
        piece_copy(d).wait_send()
        q_copy(d).wait_send()
    z_copy().wait_send()
    for t in (0, 1):
        for d in (1, -1):
            first_copy(t, d).wait_send()
            first_forward(t, d).wait_send()

        @pl.loop(0, 4)
        def _(i):
            for d in (1, -1):
                second_copy(t, i, d).wait_send()
                second_forward(t, i, d).wait_send()
            for p in range(4):
                core_copy(t, p, i).wait_send()
    for c in range(len(tails)):
        own_copy(c).wait()
        for d in (1, 2, 3):
            o_copy(d, c, hd).wait_send()
            o_copy(d, c, (hd + 4 - d) % 4).wait_recv()


def attention(shifted, queries, keys, values, positions):
    vmem = pl.BlockSpec(memory_space=pltpu.VMEM)
    anywhere = pl.BlockSpec(memory_space=pl.ANY)
    dma = pltpu.SemaphoreType.DMA
    wide = NBLK * SPAN
    table = rope_table(HEAD_DIM)
    table = jnp.asarray(np.tile(np.concatenate([table, table])[None], (8, 1)))
    return pl.pallas_call(
        functools.partial(fused, shifted),
        out_shape=(
            jax.ShapeDtypeStruct((PART, QHEADS * HEAD_DIM), BF16),
            jax.ShapeDtypeStruct((1, 1), jnp.int32),
        ),
        in_specs=[anywhere] * 5,
        out_specs=(anywhere, pl.BlockSpec(memory_space=pltpu.SMEM)),
        scratch_shapes=[
            pltpu.VMEM((PART, QHEADS * HEAD_DIM), BF16),
            pltpu.VMEM((PART, KVHEADS * HEAD_DIM), BF16),
            pltpu.VMEM((PART, KVHEADS * HEAD_DIM), BF16),
            pltpu.SMEM((PART,), jnp.int32),
            pltpu.VMEM((8, HEAD_DIM), F32),
            pltpu.VMEM((64, ROWS, HEAD_DIM), BF16),
            pltpu.VMEM((4, PIECE, HEAD_DIM), BF16),
            pltpu.VMEM((4, PIECE, HEAD_DIM), BF16),
            pltpu.VMEM((4, GROUP * PART, HEAD_DIM), BF16),
            pltpu.VMEM((4, GROUP * PART, HEAD_DIM), BF16),
            pltpu.VMEM((2 * HEAD_DIM, COLS), BF16),
            pltpu.VMEM((2, wide, HEAD_DIM), BF16),
            pltpu.VMEM((2, wide, 2 * HEAD_DIM), BF16),
            pltpu.VMEM((2, SPAN + EXTRA, wide), BF16),
            pltpu.VMEM((2, 2 * SPAN + EXTRA, wide), BF16),
            pltpu.VMEM((2, NBLK, EXTRA, HEAD_DIM), F32),
            pltpu.VMEM((SPAN + 8, COLS), F32),
            pltpu.VMEM((SPAN + 8, COLS), F32),
            pltpu.VMEM((8, COLS), F32),
            pltpu.VMEM((8, COLS), F32),
            pltpu.VMEM((4, PART, COLS), BF16),
            dma((5,)), dma((3,)), dma((3,)), dma((3,)), dma((3,)),
            dma((4, COLS // TAIL)), dma((3, COLS // TAIL)),
            dma((32, 2)), dma((32,)), dma((32,)), dma((8,)), dma((32,)), dma((1,)),
        ],
        compiler_params=pltpu.CompilerParams(
            collective_id=int(shifted), has_side_effects=True, vmem_limit_bytes=48 * 1024 * 1024
        ),
    )(queries, keys, values, positions, table)


def body(queries, keys, values, positions):
    quick, fine = attention(False, queries, keys, values, positions)
    return lax.cond(
        fine[0, 0] == 1,
        lambda: quick,
        lambda: attention(True, queries, keys, values, positions)[0],
    )


def solution(mesh):
    return jax.shard_map(
        body,
        mesh=mesh,
        in_specs=(
            P(("blk", "head"), None),
            P(("blk", "head"), None),
            P(("blk", "head"), None),
            P(("blk", "head")),
        ),
        out_specs=P(("blk", "head"), None),
        check_vma=False,
    )
```

time: 441 us -> 201 us (0.46)
  waiting for transfers between devices: 226 us -> 0 us
  Pallas kernels: 0 us -> 197 us
  matrix products: 59.2 us -> 0 us
  other arithmetic: 49 us -> 0 us
  blocking collectives: 31.1 us -> 0 us
  local copies, waits for them, and re-layouts: 25.6 us -> 1.47 us
  loops' own time: 22 us -> 0.02 us
  between operations: 15 us -> 0.76 us
  starting transfers between devices: 12 us -> 0 us
    unnamed x4 -> x0, waiting for transfers between devices: 219 us -> none
    pallas_call x0 -> x2, Pallas kernels: none -> 197 us  [attention(): pl.pallas_call(functools.partial(fused, shifted), out_shape=(jax.ShapeDty...]
    dot_general x32 -> x0, matrix products: 59.2 us -> none  [the longest x16 37.4 us: attend(): jnp.einsum('grqk,kgd->grqd', weights.astype(jnp.bfloat16), value_rows, pr...]
    all_to_all x2 -> x0, blocking collectives: 31.1 us -> none  [the longest x1 19.8 us: body(): lax.all_to_all(mixed, 'head', split_axis=0, concat_axis=1, tiled=True)]
    reduce_sum x16 -> x0, other arithmetic: 27.4 us -> none  [attend(): total = total * factor + jnp.sum(weights, axis=3)]
    another operation x17 -> x1, loops' own time: 22 us -> 0.02 us  [body(): lax.cond(fine[0, 0] == 1, lambda: quick, lambda: attention(True, queries,...]
    dynamic_slice x9 -> x0, local copies, waits for them, and re-layouts: 17.3 us -> none  [the longest x8 16.5 us: inner(): value_block = lax.dynamic_slice_in_dim(value_part, begin, step_rows, 0)]
    all_to_all x2 -> x0, starting transfers between devices: 11.9 us -> none  [the longest x1 8.46 us: body(): lax.all_to_all(values, 'head', split_axis=1, concat_axis=0, tiled=True)]
  transfers between devices with their start and end apart: 5 -> 0, of which waited for: 2 -> 0; matrix products, arithmetic and copies ran while one was open for 2% -> 0% of each run, Pallas kernels for 0% -> 0%
where the time goes in v1:
time: 201 us; the launch traced here: 199 us
  Pallas kernels  197 us (98%)
    pallas_call x2, Pallas kernels, attention(): pl.pallas_call(functools.partial(fused, shifted), out_shape=(jax.ShapeDty...  197 us

profile of v1, /device:TPU:18, one launch (start us, length us, event | category | flops | bytes accessed | tf_op | source)
XLA Modules:
  0.0 199.0 jit_solution(3666503769745042760)
XLA Ops:
  0.0 0.0 copy-start.4
  0.0 0.0 copy-start
  0.0 0.7 copy-done.4
  0.7 0.0 copy-start.1
  0.7 0.0 copy-start.2
  0.7 64.2 %shard_map.66 = (bf16[64,4096]{1,0:T(8,128)(2,1)S(1)}, s32[1,1]{1,0:T(1,128)}) custom-call(bf16[64,4096]{1,0:T(8,128)(2,1)} %q_hbm.1, bf16[64,512]{1,0:T(8,128)(2,1)} %k_hbm.1, bf16[64,512]{1,0:T(8,128)(2,1)} %v_hbm.1, s32[64]{0:T(128)S(1)} %copy-done.4, f32[8,128]{1,0:T(8,128)} %constant.5.clone.table_hbm), custom_call_target="tpu_custom_call" | custom-call | tf_op jit(solution)/shard_map/pallas_call | solution.py:488
  64.8 0.0 copy-start.3
  65.5 0.0 copy-done
  65.5 0.0 copy-done.1
  65.6 0.0 copy-done.2
  65.6 0.0 copy-done.3
  65.6 132.6 %conditional.1 = (bf16[64,4096]{1,0:T(8,128)(2,1)S(1)}) conditional(s32[]{:T(128)} %bitcast, (bf16[64,4096]{1,0:T(8,128)(2,1)S(1)}, bf16[64,512]{1,0:T(8,128)(2,1)S(1)}, bf16[64,512]{1,0:T(8,128)(2,1)S(1)}, s32[64]{0:T(128)S(1)}, f32[8,128]{1,0:T(8,128)S(1)}) %tuple.21, bf16[64,4096]{1,0:T(8,128)(2,1)S(1)} %get-tuple-element.28), branch_computations={%region_0.0_spmd, %region_1.0_spmd} | conditional | bytes 8 | solution.py:530
  65.6 132.6 %branch_0_fun.1 = (bf16[64,4096]{1,0:T(8,128)(2,1)S(1)}, s32[1,1]{1,0:T(1,128)}) custom-call(bf16[64,4096]{1,0:T(8,128)(2,1)S(1)} %get-tuple-element.19.q_hbm, bf16[64,512]{1,0:T(8,128)(2,1)S(1)} %get-tuple-element.20.k_hbm, bf16[64,512]{1,0:T(8,128)(2,1)S(1)} %get-tuple-element.21.v_hbm, s32[64]{0:T(128)S(1)} %get-tuple-element.22.pos_hbm, ...), custom_call_target="tpu_custom_call" | custom-call | tf_op jit(solution)/shard_map/cond/branch_0_fun/pallas_call | solution.py:488
  198.2 0.8 copy.12
Async XLA Ops:
  0.0 0.7 copy-start.4
  0.0 65.5 %copy-start = (bf16[64,4096]{1,0:T(8,128)(2,1)S(1)}, bf16[64,4096]{1,0:T(8,128)(2,1)}, u32[]{:S(2)}) copy-start(bf16[64,4096]{1,0:T(8,128)(2,1)} %q_hbm.1) | copy-start | bytes 1572868
  0.7 64.9 %copy-start.1 = (bf16[64,512]{1,0:T(8,128)(2,1)S(1)}, bf16[64,512]{1,0:T(8,128)(2,1)}, u32[]{:S(2)}) copy-start(bf16[64,512]{1,0:T(8,128)(2,1)} %k_hbm.1) | copy-start | bytes 196612
  0.7 64.9 %copy-start.2 = (bf16[64,512]{1,0:T(8,128)(2,1)S(1)}, bf16[64,512]{1,0:T(8,128)(2,1)}, u32[]{:S(2)}) copy-start(bf16[64,512]{1,0:T(8,128)(2,1)} %v_hbm.1) | copy-start | bytes 196612
  64.8 0.7 copy-start.3

commit v2 on v1

--- a/solution.py
+++ b/solution.py
@@ -57,9 +57,9 @@
     q_hbm, k_hbm, v_hbm, pos_hbm, table_hbm,
     out_ref, ok_ref,
     q_ref, k_ref, v_ref, pos_ref, table_ref,
-    kv, piece_out, piece_in, q_out, q_in, qc, ka, kc, va, vc, flags,
+    kv, piece_out, piece_in, layer_in, q_out, q_in, qc, ka, kc, va, vc, flags,
     acc_lo, acc_hi, top_lo, top_hi, o_out,
-    in_sem, p_ss, p_rs, q_ss, q_rs, o_ss, o_rs, rs, rsc, ss_core, ss1, ss2, ss_z,
+    in_sem, p_ss, p_rs, q_ss, q_rs, o_ss, o_rs, rs, rsc, ss_core, ss1, ss2, l_ss, l_rs,
 ):
     blk = lax.axis_index("blk")
     hd = lax.axis_index("head")
@@ -81,6 +81,7 @@
         pl.semaphore_signal(barrier, inc=1, device_id=(peer, hd), device_id_type=MESH)
     for d in (1, 2, 3):
         pl.semaphore_signal(barrier, inc=1, device_id=(blk, (hd + d) % 4), device_id_type=MESH)
+        pl.semaphore_signal(barrier, inc=1, device_id=(zn, (hd + d) % 4), device_id_type=MESH)
 
     loads = [
         pltpu.make_async_copy(a, b, in_sem.at[n])
@@ -120,7 +121,7 @@
         piece_out[g, 0:PART] = turn(k_ref[:, cols].astype(F32), cosine, sine).astype(BF16)
         piece_out[g, PART : 2 * PART] = v_ref[:, cols]
         piece_out[g, 2 * PART : PIECE] = ext
-    pl.semaphore_wait(barrier, 9)
+    pl.semaphore_wait(barrier, 12)
 
     def piece_copy(d):
         tgt = (hd + d) % 4
@@ -129,8 +130,24 @@
             send_sem=p_ss.at[d - 1], recv_sem=p_rs.at[d - 1],
             device_id=(blk, tgt), device_id_type=MESH)
 
+    def layer_copy(d):
+        tgt = (hd + d) % 4
+        return pltpu.make_async_remote_copy(
+            src_ref=piece_out.at[tgt], dst_ref=layer_in.at[hd],
+            send_sem=l_ss.at[d], recv_sem=l_rs.at[d],
+            device_id=(zn, tgt), device_id_type=MESH)
+
+    def recv_layer(d):
+        src = (hd + 4 - d) % 4
+        pltpu.make_async_remote_copy(
+            src_ref=piece_out.at[src], dst_ref=layer_in.at[src],
+            send_sem=l_ss.at[d], recv_sem=l_rs.at[d],
+            device_id=(zn, src), device_id_type=MESH).wait_recv()
+
     for d in (2, 1, 3):
         piece_copy(d).start()
+    for d in (2, 1, 3, 0):
+        layer_copy(d).start()
     piece_in[hd] = piece_out[hd]
 
     for g in range(KVHEADS):
@@ -163,27 +180,29 @@
     for d in (1, 2, 3):
         recv_piece(d)
 
-    e = [piece_in[h, 2 * PART : PIECE].astype(F32) for h in range(4)]
-    s0, s1 = e[0][0:1], e[2][0:1]
-    low_first = s0 < s1
-    mine = jnp.minimum(s0, s1)
-    qn = jnp.maximum(jnp.maximum(e[0][4:5], e[1][4:5]), jnp.maximum(e[2][4:5], e[3][4:5]))
-    kn = jnp.maximum(jnp.maximum(e[0][8:9], e[1][8:9]), jnp.maximum(e[2][8:9], e[3][8:9]))
-    pick = jnp.broadcast_to(low_first, (SPAN, HEAD_DIM))
-
     def spans(load):
         first = jnp.concatenate([load(0), load(1)], axis=0).astype(F32)
         second = jnp.concatenate([load(2), load(3)], axis=0).astype(F32)
         return first, second
 
-    k0, k1 = spans(lambda h: piece_in[h, 0:PART])
-    v0, v1 = spans(lambda h: piece_in[h, PART : 2 * PART])
-    v0, v1 = v0.T, v1.T
-    kv[blk, 0:SPAN] = jnp.where(pick, k0, k1).astype(BF16)
-    kv[blk, SPAN : 2 * SPAN] = jnp.where(pick, k1, k0).astype(BF16)
-    kv[blk, 2 * SPAN : 3 * SPAN] = jnp.where(pick, v0, v1).astype(BF16)
-    kv[blk, 3 * SPAN : 4 * SPAN] = jnp.where(pick, v1, v0).astype(BF16)
-    kv[blk, 4 * SPAN : ROWS] = extras(mine, qn, kn)
+    def assemble(pieces, b):
+        e = [pieces[h, 2 * PART : PIECE].astype(F32) for h in range(4)]
+        s0, s1 = e[0][0:1], e[2][0:1]
+        least = jnp.minimum(s0, s1)
+        qn = jnp.maximum(jnp.maximum(e[0][4:5], e[1][4:5]), jnp.maximum(e[2][4:5], e[3][4:5]))
+        kn = jnp.maximum(jnp.maximum(e[0][8:9], e[1][8:9]), jnp.maximum(e[2][8:9], e[3][8:9]))
+        low_first = jnp.broadcast_to(s0 < s1, (SPAN, HEAD_DIM))
+        k0, k1 = spans(lambda h: pieces[h, 0:PART])
+        v0, v1 = spans(lambda h: pieces[h, PART : 2 * PART])
+        v0, v1 = v0.T, v1.T
+        kv[b, 0:SPAN] = jnp.where(low_first, k0, k1).astype(BF16)
+        kv[b, SPAN : 2 * SPAN] = jnp.where(low_first, k1, k0).astype(BF16)
+        kv[b, 2 * SPAN : 3 * SPAN] = jnp.where(low_first, v0, v1).astype(BF16)
+        kv[b, 3 * SPAN : 4 * SPAN] = jnp.where(low_first, v1, v0).astype(BF16)
+        kv[b, 4 * SPAN : ROWS] = extras(least, qn, kn)
+        return least, low_first
+
+    mine, pick = assemble(piece_in, blk)
 
     def slot(t, p, i, c):
         x = xx + (1 - t) * i + t * p
@@ -214,11 +233,6 @@
         pltpu.make_async_remote_copy(
             src_ref=ref, dst_ref=ref, send_sem=ss_core.at[rid(t, p, i)],
             recv_sem=rsc.at[rid(t, p, i)], device_id=(cn, hd), device_id_type=MESH).wait_recv()
-
-    def z_copy():
-        return pltpu.make_async_remote_copy(
-            src_ref=kv.at[blk], dst_ref=kv.at[blk], send_sem=ss_z.at[0],
-            recv_sem=rs.at[rid(1, 0, 0), 0], device_id=(zn, hd), device_id_type=MESH)
 
     def first_copy(t, d):
         return copy(t, 0, 0, 0, ROWS, near(t, 0, d), ss1.at[t * 4 + (0 if d == 1 else 1)],
@@ -258,29 +272,32 @@
             second_forward(t, i, 1 if p == 3 else -1).start()
         core_copy(t, p, i).start()
 
-    def spread(t, i):
-        second(t, i)
-        core_copy(t, 0, i).start()
-
-    z_copy().start()
     for d in (1, -1):
         first_copy(0, d).start()
-    spread(0, 0)
-    recv_full(1, 0, 0)
+    for d in range(4):
+        recv_layer(d)
+    assemble(layer_in, zn)
     for d in (1, -1):
         first_copy(1, d).start()
-    spread(1, 0)
+    for t in (0, 1):
+        second(t, 0)
+        core_copy(t, 0, 0).start()
     for d in (2, 1, 3):
         q_copy(d).start()
     q_in[hd] = q_out[hd]
     for t in (0, 1):
         for d in (1, -1):
-            recv_full(t, 0, 3 if d == 1 else 1)
+            i = 3 if d == 1 else 1
+            recv_full(t, 0, i)
             first_forward(t, d).start()
-            spread(t, 3 if d == 1 else 1)
+            core_copy(t, 0, i).start()
+    for i in (3, 1):
+        for t in (0, 1):
+            second(t, i)
     for t in (0, 1):
         recv_halves(t, 0, 2)
-        spread(t, 2)
+        second(t, 2)
+        core_copy(t, 0, 2).start()
 
     acc_lo[...] = jnp.zeros_like(acc_lo)
     acc_hi[...] = jnp.zeros_like(acc_hi)
@@ -432,14 +449,16 @@
         for task in tasks:
             arrive(*task)
 
+    take(ring(0, 3)[:1] + ring(0, 1)[:1] + ring(1, 3)[:1] + ring(1, 1)[:1])
     prepare_queries()
     diagonal()
     stage(0, 0, 0)
-    take(ring(0, 3) + ring(0, 1) + ring(1, 3) + ring(1, 1))
+    take(ring(0, 3)[1:] + ring(0, 1)[1:] + ring(1, 3)[1:] + ring(1, 1)[1:])
     stage(1, 0, 1)
     stage(0, 3, 0)
     stage(1, 3, 1)
-    take(ring(0, 2) + ring(1, 2))
+    take(ring(0, 2))
+    take(ring(1, 2))
     stage(0, 1, 0)
     stage(1, 1, 1)
     gather_stage(0, 2, 0)
@@ -458,7 +477,8 @@
     for d in (1, 2, 3):
         piece_copy(d).wait_send()
         q_copy(d).wait_send()
-    z_copy().wait_send()
+    for d in range(4):
+        layer_copy(d).wait_send()
     for t in (0, 1):
         for d in (1, -1):
             first_copy(t, d).wait_send()
@@ -502,6 +522,7 @@
             pltpu.VMEM((64, ROWS, HEAD_DIM), BF16),
             pltpu.VMEM((4, PIECE, HEAD_DIM), BF16),
             pltpu.VMEM((4, PIECE, HEAD_DIM), BF16),
+            pltpu.VMEM((4, PIECE, HEAD_DIM), BF16),
             pltpu.VMEM((4, GROUP * PART, HEAD_DIM), BF16),
             pltpu.VMEM((4, GROUP * PART, HEAD_DIM), BF16),
             pltpu.VMEM((2 * HEAD_DIM, COLS), BF16),
@@ -517,7 +538,7 @@
             pltpu.VMEM((4, PART, COLS), BF16),
             dma((5,)), dma((3,)), dma((3,)), dma((3,)), dma((3,)),
             dma((4, COLS // TAIL)), dma((3, COLS // TAIL)),
-            dma((32, 2)), dma((32,)), dma((32,)), dma((8,)), dma((32,)), dma((1,)),
+            dma((32, 2)), dma((32,)), dma((32,)), dma((8,)), dma((32,)), dma((4,)), dma((4,)),
         ],
         compiler_params=pltpu.CompilerParams(
             collective_id=int(shifted), has_side_effects=True, vmem_limit_bytes=48 * 1024 * 1024

time: 201 us -> 198 us (0.985)
  Pallas kernels: 197 us -> 192 us
    pallas_call x2, Pallas kernels: 197 us -> 192 us  [attention(): pl.pallas_call(functools.partial(fused, shifted), out_shape=(jax.ShapeDty...]
where the time goes in v2:
time: 198 us; the launch traced here: 194 us
  Pallas kernels  192 us (97%)
    pallas_call x2, Pallas kernels, attention(): pl.pallas_call(functools.partial(fused, shifted), out_shape=(jax.ShapeDty...  192 us

profile of v2, /device:TPU:18, one launch (start us, length us, event | category | flops | bytes accessed | tf_op | source)
XLA Modules:
  0.0 194.5 jit_solution(914428130071342828)
XLA Ops:
  0.0 0.0 copy-start.4
  0.0 0.0 copy-start
  0.0 0.7 copy-done.4
  0.7 0.0 copy-start.1
  0.7 0.0 copy-start.2
  0.7 62.8 %shard_map.66 = (bf16[64,4096]{1,0:T(8,128)(2,1)S(1)}, s32[1,1]{1,0:T(1,128)}) custom-call(bf16[64,4096]{1,0:T(8,128)(2,1)} %q_hbm.1, bf16[64,512]{1,0:T(8,128)(2,1)} %k_hbm.1, bf16[64,512]{1,0:T(8,128)(2,1)} %v_hbm.1, s32[64]{0:T(128)S(1)} %copy-done.4, f32[8,128]{1,0:T(8,128)} %constant.5.clone.table_hbm), custom_call_target="tpu_custom_call" | custom-call | tf_op jit(solution)/shard_map/pallas_call | solution.py:508
  63.5 0.0 copy-start.3
  64.2 0.0 copy-done
  64.2 0.0 copy-done.1
  64.2 0.0 copy-done.2
  64.2 0.0 copy-done.3
  64.2 129.4 %conditional.1 = (bf16[64,4096]{1,0:T(8,128)(2,1)S(1)}) conditional(s32[]{:T(128)} %bitcast, (bf16[64,4096]{1,0:T(8,128)(2,1)S(1)}, bf16[64,512]{1,0:T(8,128)(2,1)S(1)}, bf16[64,512]{1,0:T(8,128)(2,1)S(1)}, s32[64]{0:T(128)S(1)}, f32[8,128]{1,0:T(8,128)S(1)}) %tuple.21, bf16[64,4096]{1,0:T(8,128)(2,1)S(1)} %get-tuple-element.28), branch_computations={%region_0.0_spmd, %region_1.0_spmd} | conditional | bytes 8 | solution.py:551
  64.2 129.4 %branch_0_fun.1 = (bf16[64,4096]{1,0:T(8,128)(2,1)S(1)}, s32[1,1]{1,0:T(1,128)}) custom-call(bf16[64,4096]{1,0:T(8,128)(2,1)S(1)} %get-tuple-element.19.q_hbm, bf16[64,512]{1,0:T(8,128)(2,1)S(1)} %get-tuple-element.20.k_hbm, bf16[64,512]{1,0:T(8,128)(2,1)S(1)} %get-tuple-element.21.v_hbm, s32[64]{0:T(128)S(1)} %get-tuple-element.22.pos_hbm, ...), custom_call_target="tpu_custom_call" | custom-call | tf_op jit(solution)/shard_map/cond/branch_0_fun/pallas_call | solution.py:508
  193.7 0.8 copy.12
Async XLA Ops:
  0.0 0.7 copy-start.4
  0.0 64.2 %copy-start = (bf16[64,4096]{1,0:T(8,128)(2,1)S(1)}, bf16[64,4096]{1,0:T(8,128)(2,1)}, u32[]{:S(2)}) copy-start(bf16[64,4096]{1,0:T(8,128)(2,1)} %q_hbm.1) | copy-start | bytes 1572868
  0.7 63.5 %copy-start.1 = (bf16[64,512]{1,0:T(8,128)(2,1)S(1)}, bf16[64,512]{1,0:T(8,128)(2,1)}, u32[]{:S(2)}) copy-start(bf16[64,512]{1,0:T(8,128)(2,1)} %k_hbm.1) | copy-start | bytes 196612
  0.7 63.6 %copy-start.2 = (bf16[64,512]{1,0:T(8,128)(2,1)S(1)}, bf16[64,512]{1,0:T(8,128)(2,1)}, u32[]{:S(2)}) copy-start(bf16[64,512]{1,0:T(8,128)(2,1)} %v_hbm.1) | copy-start | bytes 196612
  63.5 0.7 copy-start.3
